TPU v7x, 128 devices: a whole 4x4x4 slice. The times are simulated.
128 devices in a mesh: tm: 64 (over y, x, z), head: 2 (over core).
Axes of the slice: x: 4, y: 4, z: 4, core: 2. Of those that a mesh axis runs over, the one named last changes fastest.
Arguments:
- frames: bfloat16 [65536, 1024], P(('tm', 'head')), may hold values from -6 to 6
- conv_in: bfloat16 [1024, 2048], replicated, may hold values from -0.1875 to 0.1875
- depth_taps: float32 [31, 1024], replicated, may hold values from -1 to 1
- conv_out: bfloat16 [1024, 1024], replicated, may hold values from -0.1875 to 0.1875
- w_query: bfloat16 [1024, 1024], P(None, 'head'), may hold values from -0.1875 to 0.1875
- w_key: bfloat16 [1024, 1024], P(None, 'head'), may hold values from -0.1875 to 0.1875
- w_value: bfloat16 [1024, 1024], P(None, 'head'), may hold values from -0.1875 to 0.1875
- feature_map: bfloat16 [8, 128, 256], P('head'), may hold values from -0.5 to 0.5
- w_out: bfloat16 [1024, 1024], P('head'), may hold values from -0.1875 to 0.1875
Outputs:
- encoded: bfloat16 [65536, 1024], P(('tm', 'head'))
All inputs are finite; a program needn't handle non-finite values.
Results may differ from a plain program's by a relative error of at most 0.0085.
Values may be sent and summed in bfloat16 or wider, within the bound.
A program may use at most 128 MiB of HBM per device.

v0:
```python
import jax
import jax.numpy as jnp
from jax import lax
from jax.sharding import Mesh
from jax.sharding import PartitionSpec as P

BLK = 512
TM_HEAD = ("tm_0", "tm_1", "tm_2", "head")
TM = ("tm_0", "tm_1", "tm_2")


def padded_2(array, sides, width):
    edges = {}
    for axis, dim in sides:
        devices, length = (lax.axis_size(axis), array.shape[dim])
        up = [(i, (i + 1) % devices) for i in range(devices - 1)]
        last = lax.slice_in_dim(array, length - width, length, axis=dim)
        initial = lax.slice_in_dim(array, 0, width, axis=dim)
        edges[dim] = (
            lax.ppermute(last, axis, up),
            lax.ppermute(initial, axis, [(b, a) for a, b in up]),
        )
    done = []
    for _, dim in sides:
        low, high = edges[dim]
        around = [(width, width) if d in done else (0, 0) for d in range(array.ndim)]
        array = jnp.concatenate([jnp.pad(low, around), array, jnp.pad(high, around)], axis=dim)
        done.append(dim)
    return array


def laid_out(parts, dim):
    parts = jnp.moveaxis(parts, 0, dim)
    lengths = parts.shape
    return parts.reshape(*lengths[:dim], lengths[dim] * lengths[dim + 1], *lengths[dim + 2 :])


def from_everyone(array, axis):
    copies = jnp.broadcast_to(array, (lax.axis_size(axis), *array.shape))
    return lax.all_to_all(copies, axis, split_axis=0, concat_axis=0, tiled=True)


def gathered_copies(array, axis, dim):
    return laid_out(from_everyone(array, axis), dim)


def filled_with(array, identity):
    return jnp.broadcast_to(jnp.asarray(identity, array.dtype), array.shape)


def entering(array, axes, combine, identity):
    before = start = filled_with(array, identity)
    total = array
    for axis in reversed(axes):
        devices, index = (lax.axis_size(axis), lax.axis_index(axis))
        pieces = lax.all_gather(total.astype(jnp.bfloat16), axis)
        inside, total = (start, start)
        for k in range(devices):
            passed = k < index
            total = combine(total, pieces[k].astype(array.dtype))
            inside = jnp.where(passed, total, inside)
        before = combine(inside, before)
    return before


def split_up(array, dim, devices):
    before, after = (array.shape[:dim], array.shape[dim + 1 :])
    return jnp.moveaxis(array.reshape(*before, devices, -1, *after), dim, 0)


def sent_and_summed(array, axis, dim):
    devices = lax.axis_size(axis)
    parts = lax.all_to_all(split_up(array, dim, devices), axis, 0, 0, tiled=True)
    return jnp.sum(parts.astype(jnp.float32), axis=0)


def layer_norm(values):
    center = values - jnp.mean(values, axis=-1, keepdims=True)
    spread = jnp.mean(center * center, axis=-1, keepdims=True)
    return center * lax.rsqrt(spread + 1e-05)


def add_states(earlier, later):
    return earlier + later


def shards(frames, conv_in, depth_taps, conv_out, w_query, w_key, w_value, feature_map, w_out):
    local_rows = frames.shape[0]
    model_width = frames.shape[1]
    inputs = frames.astype(jnp.float32)
    normed = layer_norm(inputs).astype(jnp.bfloat16)
    projected = jnp.dot(normed, conv_in, preferred_element_type=jnp.float32)
    glu_out = (projected[:, :model_width] * jax.nn.sigmoid(projected[:, model_width:])).astype(
        jnp.bfloat16
    )
    tap_count = depth_taps.shape[0]
    reach = tap_count // 2
    padded = padded_2(glu_out, ((TM_HEAD, 0),), reach)
    depthwise = jnp.zeros((local_rows, model_width), jnp.float32)
    for offset in range(tap_count):
        depthwise = depthwise + depth_taps[offset] * padded[offset : offset + local_rows].astype(
            jnp.float32
        )
    activated = jax.nn.silu(layer_norm(depthwise)).astype(jnp.bfloat16)
    middle = (inputs + jnp.dot(activated, conv_out, preferred_element_type=jnp.float32)).astype(
        jnp.bfloat16
    )
    w_joined = jnp.concatenate([w_query, w_key, w_value], axis=1)
    attn_in = layer_norm(gathered_copies(middle, "head", 0).astype(jnp.float32)).astype(
        jnp.bfloat16
    )
    joined = jnp.dot(attn_in, w_joined, preferred_element_type=jnp.float32).astype(jnp.bfloat16)
    heads_local = feature_map.shape[0]
    head_dim = feature_map.shape[1]
    feats = feature_map.shape[2]
    inner = heads_local * head_dim
    total_rows = joined.shape[0]
    blocks = total_rows // BLK
    query = joined[:, :inner].reshape(total_rows, heads_local, head_dim)
    key = joined[:, inner : 2 * inner].reshape(total_rows, heads_local, head_dim)
    values = joined[:, 2 * inner :].reshape(blocks, BLK, heads_local, head_dim)
    query_map = jax.nn.silu(
        jnp.einsum("rhd,hdf->rhf", query, feature_map, preferred_element_type=jnp.float32)
    ).astype(jnp.bfloat16)
    key_map = jax.nn.silu(
        jnp.einsum("rhd,hdf->rhf", key, feature_map, preferred_element_type=jnp.float32)
    ).astype(jnp.bfloat16)
    query_map = query_map.reshape(blocks, BLK, heads_local, feats)
    key_map = key_map.reshape(blocks, BLK, heads_local, feats)
    states = jnp.einsum("bshf,bshd->bhfd", key_map, values, preferred_element_type=jnp.float32)
    own_state = jnp.sum(states, axis=0)
    empty = jnp.zeros_like(own_state)
    earlier = entering(own_state, TM, add_states, empty)
    running = jnp.concatenate([jnp.zeros_like(states[:1]), jnp.cumsum(states[:-1], axis=0)], axis=0)
    prefix = earlier[None] + running
    inter = jnp.einsum(
        "bthf,bhfd->bthd", query_map.astype(jnp.float32), prefix, precision=lax.Precision.HIGHEST
    )
    scores = jnp.einsum("bthf,bshf->bhts", query_map, key_map, preferred_element_type=jnp.float32)
    causal = jnp.arange(BLK)[:, None] >= jnp.arange(BLK)[None, :]
    weights = jnp.where(causal[None, None], scores, 0.0).astype(jnp.bfloat16)
    intra = jnp.einsum("bhts,bshd->bthd", weights, values, preferred_element_type=jnp.float32)
    numerator = (inter + intra).reshape(total_rows, heads_local, head_dim)
    scale = lax.rsqrt(jnp.mean(numerator * numerator, axis=-1, keepdims=True) + 1e-06)
    attended = (numerator * scale).astype(jnp.bfloat16).reshape(total_rows, inner)
    branch = sent_and_summed(
        jnp.dot(attended, w_out, preferred_element_type=jnp.float32).astype(jnp.bfloat16), "head", 0
    )
    return (middle.astype(jnp.float32) + branch).astype(jnp.bfloat16)


def solution(mesh):
    torus = Mesh(
        mesh.devices.reshape(4, 4, 4, mesh.shape["head"]), ("tm_0", "tm_1", "tm_2", "head")
    )
    in_specs = (
        P(TM_HEAD, None),
        P(),
        P(),
        P(),
        P(None, "head"),
        P(None, "head"),
        P(None, "head"),
        P("head", None, None),
        P("head", None),
    )
    out_specs = P(TM_HEAD, None)
    return jax.shard_map(
        shards, mesh=torus, in_specs=in_specs, out_specs=out_specs, check_vma=False
    )
```

profile of v0, /device:TPU:25, one launch (start us, length us, event | category | flops | bytes accessed | tf_op | source)
XLA Modules:
  0.0 168.7 jit_solution(1309429832774150855)
XLA Ops:
  6.5 0.0 copy-start
  6.5 0.0 all-gather.9.cloned.1.call-start
  6.5 1.6 convert_reduce_fusion.1
  8.1 1.6 fusion.22
  9.8 0.0 copy-done.2
  9.8 4.6 %fusion.42 = f32[512,2048]{1,0:T(8,128)S(1)} fusion(bf16[1024,2048]{1,0:T(8,128)(2,1)} %param.10, bf16[512,1024]{1,0:T(8,128)(2,1)S(1)} %copy-done.2, f32[512]{0:T(512)S(1)} %add_rsqrt_fusion.2, f32[512]{0:T(512)S(1)} %broadcast_multiply_fusion.2), kind=kOutput, calls=%fused_computation.86 | convolution fusion | flops 2149580800 | bytes 9441280 | tf_op jit(solution)/shard_map/dot_general | solution.py:92
  14.4 0.0 copy-start.8
  14.4 0.6 fusion.30
  15.0 2.6 %collective-permute-start.1 = (bf16[15,1024]{1,0:T(8,128)(2,1)S(1)}, bf16[15,1024]{1,0:T(8,128)(2,1)S(1)}, u32[]{:S(2)}, u32[]{:S(2)}) collective-permute-start(bf16[15,1024]{1,0:T(8,128)(2,1)S(1)} %get-tuple-element.11), channel_id=1, source_target_pairs={{1,0},{2,1},{3,2},{4,3},{5,4},{6,5},{7,6},{8,7},{9,8},{10,9},{11,1... | collective-permute-start | bytes 92168 | tf_op jit(solution)/shard_map/ppermute | solution.py:21
  17.6 3.4 %collective-permute-start = (bf16[15,1024]{1,0:T(8,128)(2,1)S(1)}, bf16[15,1024]{1,0:T(8,128)(2,1)S(1)}, u32[]{:S(2)}, u32[]{:S(2)}) collective-permute-start(bf16[15,1024]{1,0:T(8,128)(2,1)S(1)} %get-tuple-element.10), channel_id=1, source_target_pairs={{0,1},{1,2},{2,3},{3,4},{4,5},{5,6},{6,7},{7,8},{8,9},{9,10},{10,1... | collective-permute-start | bytes 92168 | tf_op jit(solution)/shard_map/ppermute | solution.py:20
  21.1 0.0 copy-done.8
  21.1 0.1 fusion.107
  21.2 0.0 collective-permute-done.1
  21.2 4.9 %collective-permute-done = bf16[15,1024]{1,0:T(8,128)(2,1)S(1)} collective-permute-done((bf16[15,1024]{1,0:T(8,128)(2,1)S(1)}, bf16[15,1024]{1,0:T(8,128)(2,1)S(1)}, u32[]{:S(2)}, u32[]{:S(2)}) %collective-permute-start) | collective-permute-done | bytes 30752 | tf_op jit(solution)/shard_map/ppermute | solution.py:20
  26.1 10.2 %fusion.105 = (f32[512]{0:T(512)S(1)}, f32[512,1024]{1,0:T(8,128)S(1)}) fusion(bf16[15,1024]{1,0:T(8,128)(2,1)S(1)} %collective-permute-done.1, bf16[512,1024]{1,0:T(8,128)(2,1)S(1)} %fusion.30, f32[1024]{0:T(1024)S(1)} %bitcast.149, f32[1024]{0:T(1024)S(1)} %bitcast.150, f32[1024]{0:T(1024)S(1)} %bitcast.121, f32[1024]{0:T(1024)S(1)} %bitcast.122, ...), kind=kLoop, calls=%fused_computation.186 | loop fusion | flops 95944192 | bytes 3336192 | tf_op jit(solution)/shard_map/reduce_sum | solution.py:78
  36.3 0.3 multiply_reduce_fusion.2
  36.6 0.0 copy-done
  36.6 1.4 fusion.24
  38.0 0.2 broadcast_in_dim.12
  38.3 12.0 %all_to_all.10 = bf16[2,512,1024]{2,1,0:T(8,128)(2,1)S(1)} all-to-all(bf16[2,512,1024]{2,1,0:T(8,128)(2,1)S(1)} %broadcast_in_dim.12), channel_id=1, replica_groups=mesh['tm_0'=4,'tm_1'=4,'tm_2'=4,'head'=2] {'head'}, dimensions={0} | all-to-all | bytes 4194304 | tf_op jit(solution)/shard_map/all_to_all | solution.py:40
  50.3 0.0 copy-done.3
  50.3 0.3 convert_reduce_fusion.2
  50.6 0.7 multiply_reduce_fusion
  51.4 0.0 copy-start.9
  51.4 0.0 copy-start.10
  51.4 0.0 copy-start.11
  51.4 0.5 fusion.8
  51.9 0.6 copy-done.9
  52.6 0.3 copy-done.10
  52.9 0.3 copy-done.11
  53.2 3.9 %convolution_convert_fusion = bf16[1024,1536]{1,0:T(8,128)(2,1)S(1)} fusion(bf16[1024,1024]{1,0:T(8,128)(2,1)S(1)} %fusion.8, bf16[1024,512]{1,0:T(8,128)(2,1)S(1)} %copy-done.9, bf16[1024,512]{1,0:T(8,128)(2,1)S(1)} %copy-done.10, bf16[1024,512]{1,0:T(8,128)(2,1)S(1)} %copy-done.11), kind=kOutput, calls=%fused_computation.49 | convolution fusion | flops 3232235520 | bytes 8388608 | tf_op jit(solution)/shard_map/dot_general | solution.py:112
  57.1 1.7 %slice_bitcast_fusion = (bf16[128,4,8,128]{3,2,1,0:T(8,128)(2,1)}, bf16[1024,512]{1,0:T(8,128)(2,1)S(1)}, bf16[128,4,8,128]{3,2,1,0:T(8,128)(2,1)}) fusion(bf16[1024,1536]{1,0:T(8,128)(2,1)S(1)} %convolution_convert_fusion), kind=kLoop, calls=%fused_computation.119 | loop fusion | bytes 6291456
  58.9 1.1 reshape.122
  60.0 1.6 copy.54
  61.7 0.0 copy-done.12
  61.7 2.5 %fusion.10 = bf16[1024,4,256]{2,0,1:T(8,128)(2,1)S(1)} fusion(bf16[4,128,256]{2,1,0:T(8,128)(2,1)S(1)} %copy-done.12, bf16[128,4,8,128]{3,2,1,0:T(8,128)(2,1)} %get-tuple-element.9), kind=kOutput, calls=%fused_computation.46 | convolution fusion | flops 273678336 | bytes 3407872 | tf_op jit(solution)/shard_map/rhd,hdf->rhf/dot_general | solution.py:126
  64.2 2.6 %fusion.109 = (bf16[4,256,128]{2,1,0:T(8,128)(2,1)}, f32[2,4,256,128]{3,2,1,0:T(8,128)}) fusion(bf16[2,512,4,128]{1,3,2,0:T(8,128)(2,1)S(1)} %copy.54, bf16[2,512,4,256]{3,1,0,2:T(8,128)(2,1)S(1)} %bitcast.117), kind=kOutput, calls=%fused_computation.190 | convolution fusion | flops 268566528 | bytes 4456448 | tf_op jit(solution)/shard_map/bshf,bshd->bhfd/dot_general | solution.py:130
  66.7 0.0 all-gather.9.cloned.1.call-update
  66.7 0.0 all-gather.5.cloned.1.call-start
  66.8 19.0 %all-gather.9.cloned.1.call-done = bf16[16,256,128]{2,1,0:T(8,128)(2,1)} async-done(((bf16[4,256,128]{2,1,0:T(8,128)(2,1)}), bf16[16,256,128]{2,1,0:T(8,128)(2,1)}) %all-gather.9.cloned.1.call-update) | async-done | bytes 1048592 | tf_op jit(solution)/shard_map/all_gather | solution.py:56
  85.8 2.0 %fusion.99 = bf16[1,4,256,128]{3,2,1,0:T(8,128)(2,1)} fusion(bf16[16,256,128]{2,1,0:T(8,128)(2,1)} %all-gather.9.cloned.1.call-done), kind=kLoop, calls=%fused_computation.173 | loop fusion | flops 1048576 | bytes 1310720 | tf_op jit(solution)/shard_map/convert_element_type | solution.py:56
  87.8 0.0 all-gather.5.cloned.1.call-update
  87.9 0.3 all-gather.7.cloned.1.call-start
  88.1 24.2 %all-gather.5.cloned.1.call-done = bf16[4,4,256,128]{3,2,1,0:T(8,128)(2,1)} async-done(((bf16[1,4,256,128]{3,2,1,0:T(8,128)(2,1)}), bf16[4,4,256,128]{3,2,1,0:T(8,128)(2,1)}) %all-gather.5.cloned.1.call-update) | async-done | bytes 1048592 | tf_op jit(solution)/shard_map/all_gather | solution.py:56
  112.4 2.0 %fusion.98 = bf16[1,4,256,128]{3,2,1,0:T(8,128)(2,1)} fusion(bf16[4,4,256,128]{3,2,1,0:T(8,128)(2,1)} %all-gather.5.cloned.1.call-done), kind=kLoop, calls=%fused_computation.171 | loop fusion | flops 1048576 | bytes 1310720 | tf_op jit(solution)/shard_map/convert_element_type | solution.py:56
  114.4 0.0 all-gather.7.cloned.1.call-update
  114.4 0.1 iota_compare_fusion
  114.5 1.9 %slice.432 = f32[1,4,256,128]{3,2,1,0:T(8,128)} slice(f32[2,4,256,128]{3,2,1,0:T(8,128)} %get-tuple-element.46), slice={[0:1], [0:4], [0:256], [0:128]} | slice | bytes 1048576 | tf_op jit(solution)/shard_map/slice | solution.py:134
  116.4 3.8 %fusion.11 = bf16[1024,4,256]{2,0,1:T(8,128)(2,1)} fusion(bf16[4,128,256]{2,1,0:T(8,128)(2,1)} %param.16, bf16[128,4,8,128]{3,2,1,0:T(8,128)(2,1)} %get-tuple-element.7), kind=kOutput, calls=%fused_computation.47 | convolution fusion | flops 273678336 | bytes 3407872 | tf_op jit(solution)/shard_map/rhd,hdf->rhf/dot_general | solution.py:123
  120.2 6.1 %fusion = f32[2,4,128,512]{3,2,1,0:T(8,128)} fusion(bf16[2,512,4,128]{1,3,2,0:T(8,128)(2,1)S(1)} %copy.54, pred[512,512]{1,0:T(8,128)(4,1)S(1)} %iota_compare_fusion, bf16[2,512,4,256]{3,1,0,2:T(8,128)(2,1)} %bitcast.118, bf16[2,512,4,256]{3,1,0,2:T(8,128)(2,1)} %bitcast.115), kind=kOutput, calls=%fused_computation.29 | convolution fusion | flops 1614807040 | bytes 7602176 | tf_op jit(solution)/shard_map/bhts,bshd->bthd/dot_general | solution.py:142
  126.4 11.3 %all-gather.7.cloned.1.call-done = bf16[4,4,256,128]{3,2,1,0:T(8,128)(2,1)} async-done(((bf16[1,4,256,128]{3,2,1,0:T(8,128)(2,1)}), bf16[4,4,256,128]{3,2,1,0:T(8,128)(2,1)}) %all-gather.7.cloned.1.call-update) | async-done | bytes 1048592 | tf_op jit(solution)/shard_map/all_gather | solution.py:56
  137.6 2.6 %fusion.88 = f32[4,256,128]{2,1,0:T(8,128)S(1)} fusion(bf16[4,4,256,128]{3,2,1,0:T(8,128)(2,1)} %all-gather.7.cloned.1.call-done, pred[]{:T(512)S(6)} %gt.44, pred[]{:T(512)S(6)} %gt.45, pred[]{:T(512)S(6)} %gt.46, pred[]{:T(512)S(6)} %gt.47, pred[]{:T(512)S(6)} %gt.43, pred[]{:T(512)S(6)} %gt.42, pred[]{:T(512)S(6)} %gt.41, pred[]{:T(512)S(6)} %gt.40, ...), kind=kLoop, calls=%fused_computation.158 | loop fusion | flops 4587520 | bytes 3670028 | tf_op jit(solution)/shard_map/add | solution.py:135
  140.2 0.0 copy-done.5
  140.2 0.0 copy-done.6
  140.2 5.3 %multiply_reduce_fusion.1 = (f32[2,512,4]{1,2,0:T(4,128)S(1)}, f32[2,512,4,128]{1,3,2,0:T(8,128)}) fusion(f32[2,4,128,512]{3,2,1,0:T(8,128)} %fusion, bf16[2,512,4,256]{3,1,0,2:T(8,128)(2,1)S(1)} %bitcast.116, f32[1,4,256,128]{3,2,1,0:T(8,128)S(1)} %copy-done.5, f32[4,256,128]{2,1,0:T(8,128)S(1)} %fusion.88), kind=kOutput, calls=%fused_computation.73 | convolution fusion | flops 1612443648 | bytes 7356416 | tf_op jit(solution)/shard_map/bthf,bhfd->bthd/dot_general | solution.py:136
  145.5 0.2 copy.56
  145.7 2.9 %copy.55 = f32[2,512,4,128]{3,2,1,0:T(4,128)} copy(f32[2,512,4,128]{1,3,2,0:T(8,128)} %get-tuple-element.48) | data formatting | bytes 4194304 | tf_op jit(solution)/shard_map/add | solution.py:143
  148.7 1.2 mul.480
  149.9 0.4 copy-done.1
  150.3 2.5 %convolution_convert_fusion.1 = bf16[1024,1024]{1,0:T(8,128)(2,1)S(1)} fusion(bf16[512,1024]{1,0:T(8,128)(2,1)} %param.17, f32[128,8,4,128]{3,2,1,0:T(4,128)S(1)} %bitcast.112, f32[128,8,4,128]{3,2,1,0:T(4,128)S(1)} %bitcast.113), kind=kOutput, calls=%fused_computation.79 | convolution fusion | flops 1075838976 | bytes 7340032 | tf_op jit(solution)/shard_map/dot_general | solution.py:147
  152.7 6.9 %all_to_all.11 = bf16[2,512,1024]{2,1,0:T(8,128)(2,1)S(1)} all-to-all(bf16[2,512,1024]{2,1,0:T(8,128)(2,1)S(1)} %bitcast.114), channel_id=1, replica_groups=mesh['tm_0'=4,'tm_1'=4,'tm_2'=4,'head'=2] {'head'}, dimensions={0} | all-to-all | bytes 4194304 | tf_op jit(solution)/shard_map/all_to_all | solution.py:73
  159.6 0.5 convert_reduce_fusion
  160.1 0.8 copy-done.4
  160.8 1.3 add_convert_fusion
  (20 shorter events, 0.1 us)
Async XLA Ops:
  6.5 30.1 %copy-start = (bf16[1024,1024]{1,0:T(8,128)(2,1)S(1)}, bf16[1024,1024]{1,0:T(8,128)(2,1)}, u32[]{:S(2)}) copy-start(bf16[1024,1024]{1,0:T(8,128)(2,1)} %param.12) | copy-start | bytes 6291460
  6.5 3.2 %copy-start.2 = (bf16[512,1024]{1,0:T(8,128)(2,1)S(1)}, bf16[512,1024]{1,0:T(8,128)(2,1)}, u32[]{:S(2)}) copy-start(bf16[512,1024]{1,0:T(8,128)(2,1)} %param.9) | copy-start | bytes 3145732
  6.5 79.3 %all-gather.9.cloned.1.call-start = ((), (), s32[]{:S(2)}) async-start(), calls=%async_computation.4 | async-start | bytes 1310720 | tf_op jit(solution)/shard_map/all_gather | solution.py:56
  14.4 6.7 %copy-start.8 = (f32[31,1024]{1,0:T(8,128)S(1)}, f32[31,1024]{1,0:T(8,128)}, u32[]{:S(2)}) copy-start(f32[31,1024]{1,0:T(8,128)} %param.11) | copy-start | bytes 380932
  15.0 6.2 %collective-permute-start.1 = (bf16[15,1024]{1,0:T(8,128)(2,1)S(1)}, bf16[15,1024]{1,0:T(8,128)(2,1)S(1)}, u32[]{:S(2)}, u32[]{:S(2)}) collective-permute-start(bf16[15,1024]{1,0:T(8,128)(2,1)S(1)} %get-tuple-element.11), channel_id=1, source_target_pairs={{1,0},{2,1},{3,2},{4,3},{5,4},{6,5},{7,6},{8,7},{9,8},{10,9},{11,1... | collective-permute-start | bytes 92168 | tf_op jit(solution)/shard_map/ppermute | solution.py:21
  17.6 8.5 %collective-permute-start = (bf16[15,1024]{1,0:T(8,128)(2,1)S(1)}, bf16[15,1024]{1,0:T(8,128)(2,1)S(1)}, u32[]{:S(2)}, u32[]{:S(2)}) collective-permute-start(bf16[15,1024]{1,0:T(8,128)(2,1)S(1)} %get-tuple-element.10), channel_id=1, source_target_pairs={{0,1},{1,2},{2,3},{3,4},{4,5},{5,6},{6,7},{7,8},{8,9},{9,10},{10,1... | collective-permute-start | bytes 92168 | tf_op jit(solution)/shard_map/ppermute | solution.py:20
  38.0 12.2 %copy-start.3 = (bf16[512,1024]{1,0:T(8,128)(2,1)}, bf16[512,1024]{1,0:T(8,128)(2,1)S(1)}, u32[]{:S(2)}) copy-start(bf16[512,1024]{1,0:T(8,128)(2,1)S(1)} %fusion.24) | copy-start | bytes 3145732
  51.4 1.2 copy-start.9
  51.4 1.5 copy-start.10
  51.4 1.8 %copy-start.11 = (bf16[1024,512]{1,0:T(8,128)(2,1)S(1)}, bf16[1024,512]{1,0:T(8,128)(2,1)}, u32[]{:S(2)}) copy-start(bf16[1024,512]{1,0:T(8,128)(2,1)} %param.13) | copy-start | bytes 3145732
  58.9 2.8 %copy-start.12 = (bf16[4,128,256]{2,1,0:T(8,128)(2,1)S(1)}, bf16[4,128,256]{2,1,0:T(8,128)(2,1)}, u32[]{:S(2)}) copy-start(bf16[4,128,256]{2,1,0:T(8,128)(2,1)} %param.16) | copy-start | bytes 786436
  64.2 2.6 %copy-start.7 = (bf16[1024,4,256]{2,0,1:T(8,128)(2,1)}, bf16[1024,4,256]{2,0,1:T(8,128)(2,1)S(1)}, u32[]{:S(2)}) copy-start(bf16[1024,4,256]{2,0,1:T(8,128)(2,1)S(1)} %fusion.10) | copy-start | bytes 6291460
  66.7 45.6 %all-gather.5.cloned.1.call-start = ((), (), s32[]{:S(2)}) async-start(), calls=%async_computation.2 | async-start | bytes 1310720 | tf_op jit(solution)/shard_map/all_gather | solution.py:56
  87.9 49.8 %all-gather.7.cloned.1.call-start = ((), (), s32[]{:S(2)}) async-start(), calls=%async_computation.3 | async-start | bytes 1310720 | tf_op jit(solution)/shard_map/all_gather | solution.py:56
  126.4 13.8 %copy-start.5 = (f32[1,4,256,128]{3,2,1,0:T(8,128)S(1)}, f32[1,4,256,128]{3,2,1,0:T(8,128)}, u32[]{:S(2)}) copy-start(f32[1,4,256,128]{3,2,1,0:T(8,128)} %slice.432) | copy-start | bytes 1572868
  137.6 2.6 %copy-start.6 = (bf16[1024,4,256]{2,0,1:T(8,128)(2,1)S(1)}, bf16[1024,4,256]{2,0,1:T(8,128)(2,1)}, u32[]{:S(2)}) copy-start(bf16[1024,4,256]{2,0,1:T(8,128)(2,1)} %fusion.11) | copy-start | bytes 6291460
  148.7 1.6 copy-start.1
  159.6 1.2 copy-start.4
Sparse Core Ops, SparseCore 0:
  66.9 18.9 all-gather.8
  88.0 24.3 all-gather.4
  114.5 23.0 all-gather.6
where the time goes:
time: 171 us; the launch traced here: 169 us
  waiting for transfers between devices  59.4 us (35%)
  matrix products  32.7 us (19%)
  other arithmetic  24.4 us (14%)
  blocking collectives  18.8 us (11%)
  local copies, waits for them, and re-layouts  13.6 us (8%)
  between operations  13.4 us (8%)
  starting transfers between devices  6.33 us (4%)
    all_gather x3, waiting for transfers between devices, entering(): pieces = lax.all_gather(total.astype(jnp.bfloat16), axis)  54.5 us
    reduce_sum x3, other arithmetic, layer_norm(): center = values - jnp.mean(values, axis=-1, keepdims=True)  12.1 us
    all_to_all x1, blocking collectives, from_everyone(): return lax.all_to_all(copies, axis, split_axis=0, concat_axis=0, tiled=True)  12 us
    all_to_all x1, blocking collectives, sent_and_summed(): lax.all_to_all(split_up(array, dim, devices), axis, 0, 0, tiled=True)  6.88 us
    dot_general x1, matrix products, shards(): jnp.einsum('bhts,bshd->bthd', weights, values, preferred_element_type=jnp...  6.14 us
    dot_general x1, matrix products, shards(): jnp.einsum('bthf,bhfd->bthd', query_map.astype(jnp.float32), prefix, prec...  5.25 us
    ppermute x1, waiting for transfers between devices, padded_2(): lax.ppermute(last, axis, up)  4.87 us
    dot_general x1, matrix products, shards(): projected = jnp.dot(normed, conv_in, preferred_element_type=jnp.float32)  4.63 us
  transfers between devices with their start and end apart: 5, of which 4 were waited for; matrix products, arithmetic and copies ran while one was open for 7% of the time, Pallas kernels for 0%

commit v1 on v0

v1 whole, which is shorter than its diff:
```python
import functools

import jax
import jax.numpy as jnp
from jax import lax
from jax.experimental import pallas as pl
from jax.experimental.pallas import tpu as pltpu
from jax.sharding import Mesh
from jax.sharding import PartitionSpec as P

AXES = ("tm_0", "tm_1", "tm_2", "head")
MESH = pl.DeviceIdType.MESH
BF16 = jnp.bfloat16
F32 = jnp.float32

ROWS = 512
D = 1024
HALO = 16
PAD = ROWS + 2 * HALO
HALF = 512
HEADS = 4
HD = 128
FEAT = 256
TAPS = 31
CHUNK = 256


def dot(a, b):
    return jnp.dot(a, b, preferred_element_type=F32)


def dot_nt(a, b):
    return lax.dot_general(a, b, (((1,), (1,)), ((), ())), preferred_element_type=F32)


def sigmoid(v):
    return 0.5 * jnp.tanh(0.5 * v) + 0.5


def silu(v):
    half = 0.5 * v
    return half * jnp.tanh(half) + half


def layer_norm(values):
    center = values - jnp.mean(values, axis=-1, keepdims=True)
    spread = jnp.mean(center * center, axis=-1, keepdims=True)
    return center * lax.rsqrt(spread + 1e-05)


def kernel(
    sizes,
    frames, conv_in, taps, conv_out, wq, wk, wv, fm, wo, out,
    xp, normed, w_in, tap_v, w_c, wq_v, wk_v, wv_v, fm_v, wo_v, fmt,
    glu, dw, act, mid, attn, proj, val, kmapt, num, att, acc, obuf,
    st_own, p_send, p_recv, a_send, a_recv, y_send, y_recv, r_send, r_recv, pref, q_send, q_recv,
    load_sem, halo_s, halo_r, w_s, w_r, pq_s, pq_r, a_s, a_r, y_s, y_r, r_s, r_r,
):
    ny, nx, nz = sizes
    planes = nx * nz
    count = ny * planes * 2
    y, x, z, h = [lax.axis_index(a) for a in AXES]
    plane = x * nz + z
    lin = ((y * nx + x) * nz + z) * 2 + h
    other = 1 - h
    pair = (y, x, z, other)

    def device(n):
        chip = lax.div(n, 2)
        column = lax.rem(chip, planes)
        return (lax.div(chip, planes), lax.div(column, nz), lax.rem(column, nz), lax.rem(n, 2))

    prev = device(lax.rem(lin + count - 1, count))
    following = device(lax.rem(lin + 1, count))

    def plane_peer(k):
        p = lax.rem(plane + k, planes)
        return (y, lax.div(p, nz), lax.rem(p, nz), h)

    def y_peer(k):
        return (lax.rem(y + k, ny), x, z, h)

    loads = []

    def load(src, dst):
        copy = pltpu.make_async_copy(src, dst, load_sem.at[len(loads)])
        copy.start()
        loads.append(copy)
        return copy

    ld_x = load(frames, xp.at[pl.ds(HALO, ROWS)])
    ld_in = []
    for c in range(8):
        at = (c % 2) * 4 + c // 2
        ld_in.append(load(conv_in.at[:, pl.ds(at * CHUNK, CHUNK)], w_in.at[at]))
    ld_tap = load(taps, tap_v)
    ld_c = load(conv_out, w_c)
    ld_k = load(wk, wk_v.at[h])
    ld_v = load(wv, wv_v.at[h])
    ld_f = load(fm, fm_v.at[h])
    ld_q = load(wq, wq_v.at[h])
    ld_o = load(wo, wo_v.at[h])

    barrier = pltpu.get_barrier_semaphore()

    def greet(d):
        pl.semaphore_signal(barrier, inc=1, device_id=d, device_id_type=MESH)

    greet(prev)
    greet(following)
    greet(pair)

    @pl.loop(1, planes)
    def _(k):
        greet(plane_peer(k))

    for k in range(1, ny):
        greet(y_peer(k))
    pl.semaphore_wait(barrier, 3 + planes - 1 + ny - 1)

    def remote(src, dst, s, r, d):
        return pltpu.make_async_remote_copy(
            src_ref=src, dst_ref=dst, send_sem=s, recv_sem=r, device_id=d, device_id_type=MESH
        )

    halo_low = remote(
        frames.at[pl.ds(0, HALO)], xp.at[pl.ds(HALO + ROWS, HALO)], halo_s.at[0], halo_r.at[0], prev
    )
    halo_high = remote(
        frames.at[pl.ds(ROWS - HALO, HALO)], xp.at[pl.ds(0, HALO)], halo_s.at[1], halo_r.at[1], following
    )
    halo_low.start()
    halo_high.start()
    weights = []
    for i, (src, dst) in enumerate(((wk, wk_v), (wv, wv_v), (fm, fm_v), (wq, wq_v), (wo, wo_v))):
        copy = remote(src, dst.at[h], w_s.at[i], w_r.at[i], pair)
        copy.start()
        weights.append(copy)

    ld_x.wait()

    @pl.loop(0, ROWS // 32)
    def _(i):
        at = pl.ds(pl.multiple_of(HALO + i * 32, 16), 32)
        normed[at, :] = layer_norm(xp[at, :].astype(F32)).astype(BF16)

    halo_low.wait()
    halo_high.wait()
    top = layer_norm(xp[pl.ds(0, HALO), :].astype(F32))
    normed[pl.ds(0, HALO), :] = jnp.where(lin == 0, 0.0, top).astype(BF16)
    bottom = layer_norm(xp[pl.ds(HALO + ROWS, HALO), :].astype(F32))
    normed[pl.ds(HALO + ROWS, HALO), :] = jnp.where(lin == count - 1, 0.0, bottom).astype(BF16)

    for c in range(4):
        ld_in[2 * c].wait()
        ld_in[2 * c + 1].wait()
        value = dot(normed[...], w_in[c])
        gate = dot(normed[...], w_in[4 + c])
        glu[:, c * CHUNK : (c + 1) * CHUNK] = (value * sigmoid(gate)).astype(BF16).astype(F32)

    ld_tap.wait()
    rb = 64

    @pl.loop(0, ROWS // rb)
    def _(i):
        base = pl.multiple_of(i * rb, rb)
        for c in range(D // 128):
            cols = slice(c * 128, (c + 1) * 128)
            window = glu[pl.ds(base, rb + 32), cols]
            total = None
            for r in range(8):
                part = None
                for q in range(4):
                    j = 8 * q + r - 1
                    if j < 0:
                        continue
                    term = window[8 * q : 8 * q + rb + 8] * tap_v[j : j + 1, cols]
                    part = term if part is None else part + term
                part = part[r : r + rb]
                total = part if total is None else total + part
            dw[pl.ds(base, rb), cols] = total
        act[pl.ds(base, rb), :] = silu(layer_norm(dw[pl.ds(base, rb), :])).astype(BF16)

    ld_c.wait()
    for c in range(4):
        cols = slice(c * CHUNK, (c + 1) * CHUNK)
        mid[:, cols] = (
            xp[pl.ds(HALO, ROWS), cols].astype(F32) + dot(act[...], w_c[:, cols])
        ).astype(BF16)

    @pl.loop(0, ROWS // 32)
    def _(i):
        at = pl.ds(pl.multiple_of(i * 32, 32), 32)
        attn[at, :] = layer_norm(mid[at, :].astype(F32)).astype(BF16)

    def half_states(half, emit):
        for c in range(2):
            cols = slice(c * CHUNK, (c + 1) * CHUNK)
            proj[:, cols] = dot(attn[...], wk_v[half, :, cols]).astype(BF16)
            val[half, :, cols] = dot(attn[...], wv_v[half, :, cols]).astype(BF16)
        for e in range(HEADS):
            cols = slice(e * HD, (e + 1) * HD)
            fmt[half, e] = fm_v[half, e].astype(F32).T.astype(BF16)
            kt = silu(dot_nt(fmt[half, e], proj[:, cols])).astype(BF16)
            kmapt[half, e] = kt
            emit(e, dot(kt, val[half, :, cols]))

    ld_k.wait()
    ld_v.wait()
    ld_f.wait()
    for copy in weights[:3]:
        copy.wait()

    def emit_other(e, s):
        p_send[e] = s.astype(BF16)

    def emit_own(e, s):
        st_own[e] = s

    half_states(other, emit_other)
    p_copy = remote(p_send, p_recv, pq_s.at[0], pq_r.at[0], pair)
    p_copy.start()
    half_states(h, emit_own)
    p_copy.wait()

    piece = HEADS * FEAT // planes
    per = planes // HEADS
    for e in range(HEADS):
        chip_state = (st_own[e] + p_recv[e].astype(F32)).astype(BF16)
        a_send[e * per : (e + 1) * per] = chip_state.reshape(per, piece, HD)

    def a_copy(k):
        p = lax.rem(plane + k, planes)
        return remote(a_send.at[p], a_recv.at[plane], a_s.at[k], a_r.at[k], plane_peer(k))

    @pl.loop(1, planes)
    def _(k):
        a_copy(k).start()

    a_recv[plane] = a_send[plane]

    ld_q.wait()
    ld_o.wait()
    weights[3].wait()
    weights[4].wait()

    def half_project(half):
        for c in range(2):
            cols = slice(c * CHUNK, (c + 1) * CHUNK)
            proj[:, cols] = dot(attn[...], wq_v[half, :, cols]).astype(BF16)

    side = ROWS // 2
    causal = lax.broadcasted_iota(jnp.int32, (side, side), 0) >= lax.broadcasted_iota(
        jnp.int32, (side, side), 1
    )

    def half_intra(half, qmaps):
        for e in range(HEADS):
            cols = slice(e * HD, (e + 1) * HD)
            qmaps[e] = silu(dot(proj[:, cols], fm_v[half, e])).astype(BF16)
            w00 = jnp.where(causal, dot(qmaps[e, :side], kmapt[half, e, :, :side]), 0.0).astype(BF16)
            num[half, e, :side] = dot(w00, val[half, :side, cols])
            w10 = dot(qmaps[e, side:], kmapt[half, e, :, :side]).astype(BF16)
            w11 = jnp.where(causal, dot(qmaps[e, side:], kmapt[half, e, :, side:]), 0.0).astype(BF16)
            num[half, e, side:] = dot(w10, val[half, :side, cols]) + dot(w11, val[half, side:, cols])

    q_other = att.at[0]
    q_own = att.at[1]
    half_project(other)
    half_intra(other, q_other)

    @pl.loop(1, planes)
    def _(k):
        a_copy(k).wait()

    run = a_recv[0].astype(F32)
    for p in range(1, planes):
        run = run + a_recv[p].astype(F32)
    y_send[...] = run

    def y_copy(k):
        return remote(y_send, y_recv.at[y], y_s.at[k], y_r.at[k], y_peer(k))

    for k in range(1, ny):
        y_copy(k).start()

    half_project(h)

    for k in range(1, ny):
        y_copy(k).wait()
    run = jnp.zeros((piece, HD), F32)
    for k in range(1, ny):
        src = lax.rem(y + ny - k, ny)
        run = run + jnp.where(src < y, y_recv[src], 0.0)
    for p in range(planes):
        r_send[p] = run.astype(BF16)
        run = run + a_recv[p].astype(F32)

    def r_copy(k):
        p = lax.rem(plane + k, planes)
        return remote(r_send.at[p], r_recv.at[plane], r_s.at[k], r_r.at[k], plane_peer(k))

    @pl.loop(1, planes)
    def _(k):
        r_copy(k).start()

    r_recv[plane] = r_send[plane]

    half_intra(h, q_own)

    @pl.loop(1, planes)
    def _(k):
        r_copy(k).wait()

    for e in range(HEADS):
        before = r_recv[e * per : (e + 1) * per].reshape(FEAT, HD).astype(F32)
        q_send[e] = (before + jnp.where(h == 0, st_own[e], 0.0)).astype(BF16)
        pref[e] = (before + jnp.where(h == 1, p_recv[e].astype(F32), 0.0)).astype(BF16)
    q_copy = remote(q_send, q_recv, pq_s.at[1], pq_r.at[1], pair)
    q_copy.start()

    def half_inter(half, qmaps, prefix):
        for e in range(HEADS):
            numerator = num[half, e] + dot(qmaps[e], prefix[e])
            scale = lax.rsqrt(jnp.mean(numerator * numerator, axis=-1, keepdims=True) + 1e-06)
            proj[:, e * HD : (e + 1) * HD] = (numerator * scale).astype(BF16)

    half_inter(h, q_own, pref)
    for c in range(4):
        cols = slice(c * CHUNK, (c + 1) * CHUNK)
        acc[:, cols] = mid[:, cols].astype(F32) + dot(proj[...], wo_v[h, :, cols])
    q_copy.wait()
    half_inter(other, q_other, q_recv)
    stores = []
    for c in range(4):
        cols = slice(c * CHUNK, (c + 1) * CHUNK)
        obuf[:, cols] = (acc[:, cols] + dot(proj[...], wo_v[other, :, cols])).astype(BF16)
        copy = pltpu.make_async_copy(obuf.at[:, cols], out.at[:, cols], load_sem.at[len(loads) + c])
        copy.start()
        stores.append(copy)
    for copy in stores:
        copy.wait()


def shards(sizes, *args):
    ny, nx, nz = sizes
    planes = nx * nz
    piece = HEADS * FEAT // planes
    dma = pltpu.SemaphoreType.DMA
    state = (HEADS, FEAT, HD)
    scratch = [
        pltpu.VMEM((PAD, D), BF16),
        pltpu.VMEM((PAD, D), BF16),
        pltpu.VMEM((8, D, CHUNK), BF16),
        pltpu.VMEM((TAPS, D), F32),
        pltpu.VMEM((D, D), BF16),
        pltpu.VMEM((2, D, HALF), BF16),
        pltpu.VMEM((2, D, HALF), BF16),
        pltpu.VMEM((2, D, HALF), BF16),
        pltpu.VMEM((2, HEADS, HD, FEAT), BF16),
        pltpu.VMEM((2, HALF, D), BF16),
        pltpu.VMEM((2, HEADS, FEAT, HD), BF16),
        pltpu.VMEM((PAD, D), F32),
        pltpu.VMEM((ROWS, D), F32),
        pltpu.VMEM((ROWS, D), BF16),
        pltpu.VMEM((ROWS, D), BF16),
        pltpu.VMEM((ROWS, D), BF16),
        pltpu.VMEM((ROWS, HALF), BF16),
        pltpu.VMEM((2, ROWS, HALF), BF16),
        pltpu.VMEM((2, HEADS, FEAT, ROWS), BF16),
        pltpu.VMEM((2, HEADS, ROWS, HD), F32),
        pltpu.VMEM((2, HEADS, ROWS, FEAT), BF16),
        pltpu.VMEM((ROWS, D), F32),
        pltpu.VMEM((ROWS, D), BF16),
        pltpu.VMEM(state, F32),
        pltpu.VMEM(state, BF16),
        pltpu.VMEM(state, BF16),
        pltpu.VMEM((planes, piece, HD), BF16),
        pltpu.VMEM((planes, piece, HD), BF16),
        pltpu.VMEM((piece, HD), F32),
        pltpu.VMEM((ny, piece, HD), F32),
        pltpu.VMEM((planes, piece, HD), BF16),
        pltpu.VMEM((planes, piece, HD), BF16),
        pltpu.VMEM(state, BF16),
        pltpu.VMEM(state, BF16),
        pltpu.VMEM(state, BF16),
        dma((20,)),
        dma((2,)),
        dma((2,)),
        dma((5,)),
        dma((5,)),
        dma((2,)),
        dma((2,)),
        dma((planes,)),
        dma((planes,)),
        dma((ny,)),
        dma((ny,)),
        dma((planes,)),
        dma((planes,)),
    ]
    return pl.pallas_call(
        functools.partial(kernel, sizes),
        out_shape=jax.ShapeDtypeStruct((ROWS, D), BF16),
        in_specs=[pl.BlockSpec(memory_space=pl.ANY)] * 9,
        out_specs=pl.BlockSpec(memory_space=pl.ANY),
        scratch_shapes=scratch,
        compiler_params=pltpu.CompilerParams(
            collective_id=0, has_side_effects=True, vmem_limit_bytes=60 * 1024 * 1024
        ),
        cost_estimate=pl.CostEstimate(
            flops=10_200_000_000, bytes_accessed=13_000_000, transcendentals=5_000_000
        ),
        name="block",
    )(*args)


def solution(mesh):
    side = round(mesh.shape["tm"] ** (1 / 3))
    sizes = (side, side, side)
    torus = Mesh(mesh.devices.reshape(*sizes, mesh.shape["head"]), AXES)
    rows = P(AXES, None)
    half = P(None, "head")
    in_specs = (rows, P(), P(), P(), half, half, half, P("head", None, None), P("head", None))
    return jax.shard_map(
        functools.partial(shards, sizes), mesh=torus, in_specs=in_specs, out_specs=rows, check_vma=False
    )
```

time: 171 us -> 56.2 us (0.33)
  the two profiles are of different devices: /device:TPU:25 before, /device:TPU:1 now
where the time goes in v1:
time: 56.2 us; the launch traced here: 56.1 us
  Pallas kernels  53.8 us (96%)
  local copies, waits for them, and re-layouts  2.26 us (4%)
    pallas_call x1, Pallas kernels, shards(): pl.pallas_call(functools.partial(kernel, sizes), out_shape=jax.ShapeDtype...  53.8 us
    unnamed x1, local copies, waits for them, and re-layouts  2.26 us

profile of v1, /device:TPU:1, one launch (start us, length us, event | category | flops | bytes accessed | tf_op | source)
XLA Modules:
  0.0 56.1 jit_solution(5541395208243985741)
XLA Ops:
  0.0 53.8 %block.1 = bf16[512,1024]{1,0:T(8,128)(2,1)} custom-call(bf16[512,1024]{1,0:T(8,128)(2,1)} %frames.1, bf16[1024,2048]{1,0:T(8,128)(2,1)} %conv_in.1, f32[31,1024]{1,0:T(8,128)} %taps.1, bf16[1024,1024]{1,0:T(8,128)(2,1)} %conv_out.1, bf16[1024,512]{1,0:T(8,128)(2,1)} %wq.1, bf16[1024,512]{1,0:T(8,128)(2,1)} %wk.1, bf16[1024,512]{1,0:T(8,128)(2,1)} %wv.1, ...), custom_call_target="tpu_custom_call" | custom-call | flops 10200000512 | bytes 13000000 | tf_op jit(solution)/shard_map/block/pallas_call | solution.py:401
  53.8 2.3 %copy.11 = bf16[512,1024]{1,0:T(8,128)(2,1)} copy(bf16[512,1024]{1,0:T(8,128)(2,1)} %block.1) | data formatting | bytes 2097152

commit v2 on v1

v2 whole, which is shorter than its diff:
```python
import functools

import jax
import jax.numpy as jnp
from jax import lax
from jax.experimental import pallas as pl
from jax.experimental.pallas import tpu as pltpu
from jax.sharding import Mesh
from jax.sharding import PartitionSpec as P

AXES = ("tm_0", "tm_1", "tm_2", "head")
MESH = pl.DeviceIdType.MESH
BF16 = jnp.bfloat16
F32 = jnp.float32

ROWS = 512
D = 1024
HALO = 16
PAD = ROWS + 2 * HALO
HALF = 512
HEADS = 4
HD = 128
FEAT = 256
TAPS = 31
CHUNK = 256


def dot(a, b):
    return jnp.dot(a, b, preferred_element_type=F32)


def dot_nt(a, b):
    return lax.dot_general(a, b, (((1,), (1,)), ((), ())), preferred_element_type=F32)


def sigmoid(v):
    return 0.5 * jnp.tanh(0.5 * v) + 0.5


def silu(v):
    half = 0.5 * v
    return half * jnp.tanh(half) + half


def row_stats(read):
    total = read(0)
    for c in range(1, D // 128):
        total = total + read(c)
    mean = jnp.sum(total, axis=-1, keepdims=True) * (1.0 / D)
    spread = None
    for c in range(D // 128):
        center = read(c) - mean
        spread = center * center if spread is None else spread + center * center
    return mean, lax.rsqrt(jnp.sum(spread, axis=-1, keepdims=True) * (1.0 / D) + 1e-05)


def normalize(src, first, dst):
    for i in range(ROWS // 128):
        at = pl.ds(first + i * 128, 128)

        def read(c):
            return src[at, c * 128 : (c + 1) * 128].astype(F32)

        mean, scale = row_stats(read)
        for c in range(D // 128):
            dst[i * 128 : (i + 1) * 128, c * 128 : (c + 1) * 128] = ((read(c) - mean) * scale).astype(BF16)


def gated(c, normed, w_in, glu):
    value = dot(normed[...], w_in[c])
    gate = dot(normed[...], w_in[4 + c])
    glu[HALO : HALO + ROWS, c * CHUNK : (c + 1) * CHUNK] = (
        (value * sigmoid(gate)).astype(BF16).astype(F32)
    )


def convolve(base, count, glu, tap_v, dw):
    for c in range(D // 128):
        cols = slice(c * 128, (c + 1) * 128)
        window = glu[pl.ds(base, count + 32), cols]
        total = None
        for r in range(8):
            part = None
            for q in range(4):
                j = 8 * q + r - 1
                if j < 0:
                    continue
                term = window[8 * q : 8 * q + count + 8] * tap_v[j : j + 1, cols]
                part = term if part is None else part + term
            part = part[r : r + count]
            total = part if total is None else total + part
        dw[pl.ds(base, count), cols] = total


def convolve_inner(glu, tap_v, dw):
    @pl.loop(0, 3)
    def _(i):
        convolve(pl.multiple_of(64 + i * 128, 64), 128, glu, tap_v, dw)


def convolve_edges(glu, tap_v, dw):
    @pl.loop(0, 2)
    def _(i):
        convolve(pl.multiple_of(i * (ROWS - 64), 64), 64, glu, tap_v, dw)


def activate(dw, act):
    for i in range(ROWS // 128):
        at = slice(i * 128, (i + 1) * 128)

        def read(c):
            return dw[at, c * 128 : (c + 1) * 128]

        mean, scale = row_stats(read)
        for c in range(D // 128):
            act[at, c * 128 : (c + 1) * 128] = silu((read(c) - mean) * scale).astype(BF16)


def conv_back(x, act, w_c, mid):
    for c in range(4):
        cols = slice(c * CHUNK, (c + 1) * CHUNK)
        mid[:, cols] = (x[:, cols].astype(F32) + dot(act[...], w_c[:, cols])).astype(BF16)


def key_states(half, c, attn, wk_v, wv_v, fm_v, fmt, proj, val, kmapt, emit):
    wide = slice(c * CHUNK, (c + 1) * CHUNK)
    proj[...] = dot(attn[...], wk_v[half, :, wide]).astype(BF16)
    val[half, :, wide] = dot(attn[...], wv_v[half, :, wide]).astype(BF16)
    for i in range(2):
        e = 2 * c + i
        fmt[half, e] = fm_v[half, e].astype(F32).T.astype(BF16)
        kt = silu(dot_nt(fmt[half, e], proj[:, i * HD : (i + 1) * HD])).astype(BF16)
        kmapt[half, e] = kt
        emit(e, dot(kt, val[half, :, e * HD : (e + 1) * HD]))


def intra(half, c, attn, wq_v, fm_v, proj, qmap, kmapt, val, num):
    side = ROWS // 2
    causal = lax.broadcasted_iota(jnp.int32, (side, side), 0) >= lax.broadcasted_iota(
        jnp.int32, (side, side), 1
    )
    wide = slice(c * CHUNK, (c + 1) * CHUNK)
    proj[...] = dot(attn[...], wq_v[half, :, wide]).astype(BF16)
    for i in range(2):
        e = 2 * c + i
        cols = slice(e * HD, (e + 1) * HD)
        qmap[half, e] = silu(dot(proj[:, i * HD : (i + 1) * HD], fm_v[half, e])).astype(BF16)
        w00 = jnp.where(causal, dot(qmap[half, e, :side], kmapt[half, e, :, :side]), 0.0).astype(BF16)
        num[half, e, :side] = dot(w00, val[half, :side, cols])
        w10 = dot(qmap[half, e, side:], kmapt[half, e, :, :side]).astype(BF16)
        w11 = jnp.where(causal, dot(qmap[half, e, side:], kmapt[half, e, :, side:]), 0.0).astype(BF16)
        num[half, e, side:] = dot(w10, val[half, :side, cols]) + dot(w11, val[half, side:, cols])


def inter(half, e, qmap, prefix, num, attended):
    numerator = num[half, e] + dot(qmap[half, e], prefix[e])
    scale = lax.rsqrt(jnp.mean(numerator * numerator, axis=-1, keepdims=True) + 1e-06)
    attended[:, e * HD : (e + 1) * HD] = (numerator * scale).astype(BF16)


def first_output(half, mid, attended, wo_v, acc):
    for c in range(4):
        cols = slice(c * CHUNK, (c + 1) * CHUNK)
        acc[:, cols] = mid[:, cols].astype(F32) + dot(attended[...], wo_v[half, :, cols])


def last_output(half, acc, attended, wo_v, out):
    for c in range(4):
        cols = slice(c * CHUNK, (c + 1) * CHUNK)
        out[:, cols] = (acc[:, cols] + dot(attended[...], wo_v[half, :, cols])).astype(BF16)


def kernel(
    sizes,
    frames, conv_in, taps, conv_out, wq, wk, wv, fm, wo, out,
    x_v, normed, w_in, tap_v, w_c, wq_v, wk_v, wv_v, fm_v, wo_v, fmt,
    glu, dw, act, mid, attn, proj, val, kmapt, num, qmap, acc, attended,
    st_own, p_send, p_recv, a_send, a_recv, y_send, y_recv, r_send, r_recv, pref, q_send, q_recv,
    load_sem, halo_s, halo_r, w_s, w_r, p_s, p_r, a_s, a_r, y_s, y_r, r_s, r_r, q_s, q_r,
):
    ny, nx, nz = sizes
    planes = nx * nz
    count = ny * planes * 2
    y, x, z, h = [lax.axis_index(a) for a in AXES]
    plane = x * nz + z
    lin = ((y * nx + x) * nz + z) * 2 + h
    other = 1 - h
    pair = (y, x, z, other)
    has_prev = lin > 0
    has_next = lin < count - 1

    def device(n):
        chip = lax.div(n, 2)
        column = lax.rem(chip, planes)
        return (lax.div(chip, planes), lax.div(column, nz), lax.rem(column, nz), lax.rem(n, 2))

    prev = device(lax.rem(lin + count - 1, count))
    following = device(lax.rem(lin + 1, count))

    def plane_peer(k):
        p = lax.rem(plane + k, planes)
        return (y, lax.div(p, nz), lax.rem(p, nz), h)

    loads = []

    def load(src, dst):
        copy = pltpu.make_async_copy(src, dst, load_sem.at[len(loads)])
        copy.start()
        loads.append(copy)
        return copy

    ld_x = load(frames, x_v)
    ld_in = []
    for c in range(8):
        at = (c % 2) * 4 + c // 2
        ld_in.append(load(conv_in.at[:, pl.ds(at * CHUNK, CHUNK)], w_in.at[at]))
    ld_tap = load(taps, tap_v)
    ld_c = load(conv_out, w_c)
    ld_k = load(wk, wk_v.at[h])
    ld_v = load(wv, wv_v.at[h])
    ld_f = load(fm, fm_v.at[h])
    ld_q = load(wq, wq_v.at[h])
    ld_o = load(wo, wo_v.at[h])

    barrier = pltpu.get_barrier_semaphore()

    def greet(d):
        pl.semaphore_signal(barrier, inc=1, device_id=d, device_id_type=MESH)

    @pl.when(has_prev)
    def _():
        greet(prev)

    @pl.when(has_next)
    def _():
        greet(following)

    greet(pair)

    @pl.loop(1, planes)
    def _(k):
        greet(plane_peer(k))

    for k in range(1, ny):
        greet((lax.rem(y + k, ny), x, z, h))

    def remote(src, dst, s, r, d):
        return pltpu.make_async_remote_copy(
            src_ref=src, dst_ref=dst, send_sem=s, recv_sem=r, device_id=d, device_id_type=MESH
        )

    ld_x.wait()
    normalize(x_v, 0, normed)
    for c in range(4):
        ld_in[2 * c].wait()
        ld_in[2 * c + 1].wait()
        gated(c, normed, w_in, glu)

    pl.semaphore_wait(
        barrier, 1 + planes - 1 + ny - 1 + has_prev.astype(jnp.int32) + has_next.astype(jnp.int32)
    )
    low = remote(
        glu.at[pl.ds(HALO, HALO)], glu.at[pl.ds(HALO + ROWS, HALO)], halo_s.at[0], halo_r.at[0], prev
    )
    high = remote(
        glu.at[pl.ds(ROWS, HALO)], glu.at[pl.ds(0, HALO)], halo_s.at[1], halo_r.at[1], following
    )

    @pl.when(has_prev)
    def _():
        low.start()

    @pl.when(has_next)
    def _():
        high.start()

    weights = []
    for i, (src, dst) in enumerate(((wk, wk_v), (wv, wv_v), (fm, fm_v), (wq, wq_v), (wo, wo_v))):
        copy = remote(src, dst.at[h], w_s.at[i], w_r.at[i], pair)
        copy.start()
        weights.append(copy)

    ld_tap.wait()
    convolve_inner(glu, tap_v, dw)

    @pl.when(has_prev)
    def _():
        low.wait_send()
        high.wait_recv()

    @pl.when(has_next)
    def _():
        high.wait_send()
        low.wait_recv()

    @pl.when(jnp.logical_not(has_prev))
    def _():
        glu[pl.ds(0, HALO), :] = jnp.zeros((HALO, D), F32)

    @pl.when(jnp.logical_not(has_next))
    def _():
        glu[pl.ds(HALO + ROWS, HALO), :] = jnp.zeros((HALO, D), F32)

    convolve_edges(glu, tap_v, dw)
    activate(dw, act)

    ld_c.wait()
    conv_back(x_v, act, w_c, mid)
    normalize(mid, 0, attn)

    ld_k.wait()
    ld_v.wait()
    ld_f.wait()
    for copy in weights[:3]:
        copy.wait()

    def emit_other(e, s):
        p_send[e] = s.astype(BF16)

    def emit_own(e, s):
        st_own[e] = s

    def keys(half, c, emit):
        key_states(half, c, attn, wk_v, wv_v, fm_v, fmt, proj, val, kmapt, emit)

    def queries(half, c):
        intra(half, c, attn, wq_v, fm_v, proj, qmap, kmapt, val, num)

    piece = 2 * FEAT // planes
    per = planes // 2

    def p_copy(c):
        at = pl.ds(2 * c, 2)
        return remote(p_send.at[at], p_recv.at[at], p_s.at[c], p_r.at[c], pair)

    def q_copy(c):
        at = pl.ds(2 * c, 2)
        return remote(q_send.at[at], q_recv.at[at], q_s.at[c], q_r.at[c], pair)

    def a_copy(c, k):
        p = lax.rem(plane + k, planes)
        return remote(a_send.at[c, p], a_recv.at[c, plane], a_s.at[c, k], a_r.at[c, k], plane_peer(k))

    def r_copy(c, k):
        p = lax.rem(plane + k, planes)
        return remote(r_send.at[c, p], r_recv.at[c, plane], r_s.at[c, k], r_r.at[c, k], plane_peer(k))

    def y_copy(c, k):
        return remote(
            y_send.at[c], y_recv.at[c, k], y_s.at[c, k], y_r.at[c, k], (lax.rem(y + k, ny), x, z, h)
        )

    def a_start(c):
        p_copy(c).wait()
        for i in range(2):
            e = 2 * c + i
            chip_state = (st_own[e] + p_recv[e].astype(F32)).astype(BF16)
            a_send[c, i * per : (i + 1) * per] = chip_state.reshape(per, piece, HD)

        @pl.loop(1, planes)
        def _(k):
            a_copy(c, k).start()

        a_recv[c, plane] = a_send[c, plane]

    def y_start(c):
        @pl.loop(1, planes)
        def _(k):
            a_copy(c, k).wait()

        run = a_recv[c, 0].astype(F32)
        for p in range(1, planes):
            run = run + a_recv[c, p].astype(F32)
        y_send[c] = run
        for k in range(1, ny):

            @pl.when(y + k < ny)
            def _():
                y_copy(c, k).start()

    def r_start(c):
        for k in range(1, ny):

            @pl.when(y + k < ny)
            def _():
                y_copy(c, k).wait_send()

            @pl.when(y >= k)
            def _():
                y_copy(c, k).wait_recv()

        run = jnp.zeros((piece, HD), F32)
        for k in range(1, ny):
            run = run + jnp.where(y >= k, y_recv[c, k], 0.0)
        for p in range(planes):
            r_send[c, p] = run.astype(BF16)
            run = run + a_recv[c, p].astype(F32)

        @pl.loop(1, planes)
        def _(k):
            r_copy(c, k).start()

        r_recv[c, plane] = r_send[c, plane]

    def q_start(c):
        @pl.loop(1, planes)
        def _(k):
            r_copy(c, k).wait()

        for i in range(2):
            e = 2 * c + i
            before = r_recv[c, i * per : (i + 1) * per].reshape(FEAT, HD).astype(F32)
            q_send[e] = (before + jnp.where(h == 0, st_own[e], 0.0)).astype(BF16)
            pref[e] = (before + jnp.where(h == 1, p_recv[e].astype(F32), 0.0)).astype(BF16)
        q_copy(c).start()

    keys(other, 0, emit_other)
    p_copy(0).start()
    keys(other, 1, emit_other)
    p_copy(1).start()
    keys(h, 0, emit_own)
    a_start(0)
    keys(h, 1, emit_own)
    a_start(1)
    ld_q.wait()
    ld_o.wait()
    weights[3].wait()
    weights[4].wait()
    queries(other, 0)
    y_start(0)
    queries(other, 1)
    y_start(1)
    r_start(0)
    queries(h, 0)
    r_start(1)
    queries(h, 1)
    q_start(0)
    inter(h, 0, qmap, pref, num, attended)
    inter(h, 1, qmap, pref, num, attended)
    q_start(1)
    inter(h, 2, qmap, pref, num, attended)
    inter(h, 3, qmap, pref, num, attended)
    first_output(h, mid, attended, wo_v, acc)
    for c in range(2):
        q_copy(c).wait()
        for i in range(2):
            inter(other, 2 * c + i, qmap, q_recv, num, attended)
    last_output(other, acc, attended, wo_v, out)


def shards(sizes, *args):
    ny, nx, nz = sizes
    planes = nx * nz
    piece = 2 * FEAT // planes
    dma = pltpu.SemaphoreType.DMA
    state = (HEADS, FEAT, HD)
    scratch = [
        pltpu.VMEM((ROWS, D), BF16),
        pltpu.VMEM((ROWS, D), BF16),
        pltpu.VMEM((8, D, CHUNK), BF16),
        pltpu.VMEM((TAPS, D), F32),
        pltpu.VMEM((D, D), BF16),
        pltpu.VMEM((2, D, HALF), BF16),
        pltpu.VMEM((2, D, HALF), BF16),
        pltpu.VMEM((2, D, HALF), BF16),
        pltpu.VMEM((2, HEADS, HD, FEAT), BF16),
        pltpu.VMEM((2, HALF, D), BF16),
        pltpu.VMEM((2, HEADS, FEAT, HD), BF16),
        pltpu.VMEM((PAD, D), F32),
        pltpu.VMEM((ROWS, D), F32),
        pltpu.VMEM((ROWS, D), BF16),
        pltpu.VMEM((ROWS, D), BF16),
        pltpu.VMEM((ROWS, D), BF16),
        pltpu.VMEM((ROWS, CHUNK), BF16),
        pltpu.VMEM((2, ROWS, HALF), BF16),
        pltpu.VMEM((2, HEADS, FEAT, ROWS), BF16),
        pltpu.VMEM((2, HEADS, ROWS, HD), F32),
        pltpu.VMEM((2, HEADS, ROWS, FEAT), BF16),
        pltpu.VMEM((ROWS, D), F32),
        pltpu.VMEM((ROWS, HALF), BF16),
        pltpu.VMEM(state, F32),
        pltpu.VMEM(state, BF16),
        pltpu.VMEM(state, BF16),
        pltpu.VMEM((2, planes, piece, HD), BF16),
        pltpu.VMEM((2, planes, piece, HD), BF16),
        pltpu.VMEM((2, piece, HD), F32),
        pltpu.VMEM((2, ny, piece, HD), F32),
        pltpu.VMEM((2, planes, piece, HD), BF16),
        pltpu.VMEM((2, planes, piece, HD), BF16),
        pltpu.VMEM(state, BF16),
        pltpu.VMEM(state, BF16),
        pltpu.VMEM(state, BF16),
        dma((16,)),
        dma((2,)),
        dma((2,)),
        dma((5,)),
        dma((5,)),
        dma((2,)),
        dma((2,)),
        dma((2, planes)),
        dma((2, planes)),
        dma((2, ny)),
        dma((2, ny)),
        dma((2, planes)),
        dma((2, planes)),
        dma((2,)),
        dma((2,)),
    ]
    return pl.pallas_call(
        functools.partial(kernel, sizes),
        out_shape=pltpu.VMEM((ROWS, D), BF16),
        in_specs=[pl.BlockSpec(memory_space=pl.ANY)] * 9,
        out_specs=pl.BlockSpec(memory_space=pltpu.VMEM),
        scratch_shapes=scratch,
        compiler_params=pltpu.CompilerParams(
            collective_id=0, has_side_effects=True, vmem_limit_bytes=56 * 1024 * 1024
        ),
        cost_estimate=pl.CostEstimate(
            flops=10_200_000_000, bytes_accessed=13_000_000, transcendentals=5_000_000
        ),
        name="block",
    )(*args)


def solution(mesh):
    side = round(mesh.shape["tm"] ** (1 / 3))
    sizes = (side, side, side)
    torus = Mesh(mesh.devices.reshape(*sizes, mesh.shape["head"]), AXES)
    rows = P(AXES, None)
    half = P(None, "head")
    in_specs = (rows, P(), P(), P(), half, half, half, P("head", None, None), P("head", None))
    return jax.shard_map(
        functools.partial(shards, sizes), mesh=torus, in_specs=in_specs, out_specs=rows, check_vma=False
    )
```

time: 56.2 us -> 41.3 us (0.73)
  the two profiles are of different devices: /device:TPU:1 before, /device:TPU:25 now
where the time goes in v2:
time: 41.3 us
  Pallas kernels  40.3 us (98%)
  local copies, waits for them, and re-layouts  0.97 us (2%)
    pallas_call x1, Pallas kernels, shards(): pl.pallas_call(functools.partial(kernel, sizes), out_shape=pltpu.VMEM((RO...  40.3 us
    unnamed x1, local copies, waits for them, and re-layouts  0.97 us

profile of v2, /device:TPU:25, one launch (start us, length us, event | category | flops | bytes accessed | tf_op | source)
XLA Modules:
  0.0 41.3 jit_solution(12235046364480660363)
XLA Ops:
  0.0 40.3 %block.1 = bf16[512,1024]{1,0:T(8,128)(2,1)S(1)} custom-call(bf16[512,1024]{1,0:T(8,128)(2,1)} %frames.1, bf16[1024,2048]{1,0:T(8,128)(2,1)} %conv_in.1, f32[31,1024]{1,0:T(8,128)} %taps.1, bf16[1024,1024]{1,0:T(8,128)(2,1)} %conv_out.1, bf16[1024,512]{1,0:T(8,128)(2,1)} %wq.1, bf16[1024,512]{1,0:T(8,128)(2,1)} %wk.1, bf16[1024,512]{1,0:T(8,128)(2,1)} %wv.1, ...), custom_call_target="tpu_custom_call" | custom-call | flops 10200000512 | bytes 13000000 | tf_op jit(solution)/shard_map/block/pallas_call | solution.py:509
  40.3 1.0 %copy.11 = bf16[512,1024]{1,0:T(8,128)(2,1)} copy(bf16[512,1024]{1,0:T(8,128)(2,1)S(1)} %block.1) | data formatting | bytes 2097152

commit v3 on v2

--- a/solution.py
+++ b/solution.py
@@ -54,9 +54,9 @@
     return mean, lax.rsqrt(jnp.sum(spread, axis=-1, keepdims=True) * (1.0 / D) + 1e-05)
 
 
-def normalize(src, first, dst):
-    for i in range(ROWS // 128):
-        at = pl.ds(first + i * 128, 128)
+def normalize(src, first, last, dst):
+    for i in range(first, last):
+        at = pl.ds(i * 128, 128)
 
         def read(c):
             return src[at, c * 128 : (c + 1) * 128].astype(F32)
@@ -122,16 +122,16 @@
         mid[:, cols] = (x[:, cols].astype(F32) + dot(act[...], w_c[:, cols])).astype(BF16)
 
 
-def key_states(half, c, attn, wk_v, wv_v, fm_v, fmt, proj, val, kmapt, emit):
+def key_states(half, c, attn, wk_v, wv_v, fmt, val, kmapt, emit):
     wide = slice(c * CHUNK, (c + 1) * CHUNK)
-    proj[...] = dot(attn[...], wk_v[half, :, wide]).astype(BF16)
-    val[half, :, wide] = dot(attn[...], wv_v[half, :, wide]).astype(BF16)
+    key = dot(attn[...], wk_v[half, :, wide]).astype(BF16)
+    value = dot(attn[...], wv_v[half, :, wide]).astype(BF16)
+    val[half, :, wide] = value
+    maps = [dot_nt(fmt[half, 2 * c + i], key[:, i * HD : (i + 1) * HD]) for i in range(2)]
+    maps = [silu(m).astype(BF16) for m in maps]
     for i in range(2):
-        e = 2 * c + i
-        fmt[half, e] = fm_v[half, e].astype(F32).T.astype(BF16)
-        kt = silu(dot_nt(fmt[half, e], proj[:, i * HD : (i + 1) * HD])).astype(BF16)
-        kmapt[half, e] = kt
-        emit(e, dot(kt, val[half, :, e * HD : (e + 1) * HD]))
+        kmapt[half, 2 * c + i] = maps[i]
+        emit(2 * c + i, dot(maps[i], value[:, i * HD : (i + 1) * HD]))
 
 
 def intra(half, c, attn, wq_v, fm_v, proj, qmap, kmapt, val, num):
@@ -155,19 +155,31 @@
 def inter(half, e, qmap, prefix, num, attended):
     numerator = num[half, e] + dot(qmap[half, e], prefix[e])
     scale = lax.rsqrt(jnp.mean(numerator * numerator, axis=-1, keepdims=True) + 1e-06)
-    attended[:, e * HD : (e + 1) * HD] = (numerator * scale).astype(BF16)
-
-
-def first_output(half, mid, attended, wo_v, acc):
+    attended[half, :, e * HD : (e + 1) * HD] = (numerator * scale).astype(BF16)
+
+
+def out_part(half, heads, cols, attended, wo_v):
+    part = slice(heads * CHUNK, (heads + 1) * CHUNK)
+    return dot(attended[half, :, part], wo_v[half, part, cols])
+
+
+def first_output(mid, attended, wo_v, acc):
     for c in range(4):
         cols = slice(c * CHUNK, (c + 1) * CHUNK)
-        acc[:, cols] = mid[:, cols].astype(F32) + dot(attended[...], wo_v[half, :, cols])
-
-
-def last_output(half, acc, attended, wo_v, out):
+        both = out_part(0, 0, cols, attended, wo_v) + out_part(1, 0, cols, attended, wo_v)
+        acc[:, cols] = mid[:, cols].astype(F32) + both
+
+
+def own_output(own, attended, wo_v, acc):
     for c in range(4):
         cols = slice(c * CHUNK, (c + 1) * CHUNK)
-        out[:, cols] = (acc[:, cols] + dot(attended[...], wo_v[half, :, cols])).astype(BF16)
+        acc[:, cols] += out_part(own, 1, cols, attended, wo_v)
+
+
+def last_output(other, attended, wo_v, acc, out):
+    for c in range(4):
+        cols = slice(c * CHUNK, (c + 1) * CHUNK)
+        out[:, cols] = (acc[:, cols] + out_part(other, 1, cols, attended, wo_v)).astype(BF16)
 
 
 def kernel(
@@ -184,8 +196,8 @@
     y, x, z, h = [lax.axis_index(a) for a in AXES]
     plane = x * nz + z
     lin = ((y * nx + x) * nz + z) * 2 + h
-    other = 1 - h
-    pair = (y, x, z, other)
+    other, own = 0, 1
+    pair = (y, x, z, 1 - h)
     has_prev = lin > 0
     has_next = lin < count - 1
 
@@ -209,19 +221,14 @@
         loads.append(copy)
         return copy
 
-    ld_x = load(frames, x_v)
+    ld_x = []
+    for at in (pl.ds(0, ROWS // 2), pl.ds(ROWS // 2, ROWS // 2)):
+        ld_x.append(load(frames.at[at], x_v.at[at]))
+    ld_f = load(fm, fm_v.at[own])
     ld_in = []
     for c in range(8):
         at = (c % 2) * 4 + c // 2
         ld_in.append(load(conv_in.at[:, pl.ds(at * CHUNK, CHUNK)], w_in.at[at]))
-    ld_tap = load(taps, tap_v)
-    ld_c = load(conv_out, w_c)
-    ld_k = load(wk, wk_v.at[h])
-    ld_v = load(wv, wv_v.at[h])
-    ld_f = load(fm, fm_v.at[h])
-    ld_q = load(wq, wq_v.at[h])
-    ld_o = load(wo, wo_v.at[h])
-
     barrier = pltpu.get_barrier_semaphore()
 
     def greet(d):
@@ -249,8 +256,19 @@
             src_ref=src, dst_ref=dst, send_sem=s, recv_sem=r, device_id=d, device_id_type=MESH
         )
 
-    ld_x.wait()
-    normalize(x_v, 0, normed)
+    ld_x[0].wait()
+    ld_tap = load(taps, tap_v)
+    ld_c = load(conv_out, w_c)
+    ld_k = load(wk, wk_v.at[own])
+    ld_v = load(wv, wv_v.at[own])
+    ld_q = load(wq, wq_v.at[own])
+    ld_o = load(wo, wo_v.at[own])
+    normalize(x_v, 0, 2, normed)
+    ld_x[1].wait()
+    normalize(x_v, 2, 4, normed)
+    ld_f.wait()
+    for e in range(HEADS):
+        fmt[own, e] = fm_v[own, e].astype(F32).T.astype(BF16)
     for c in range(4):
         ld_in[2 * c].wait()
         ld_in[2 * c + 1].wait()
@@ -275,8 +293,8 @@
         high.start()
 
     weights = []
-    for i, (src, dst) in enumerate(((wk, wk_v), (wv, wv_v), (fm, fm_v), (wq, wq_v), (wo, wo_v))):
-        copy = remote(src, dst.at[h], w_s.at[i], w_r.at[i], pair)
+    for i, (src, dst) in enumerate(((wk, wk_v), (wv, wv_v), (fmt.at[own], fmt), (fm, fm_v), (wq, wq_v), (wo, wo_v))):
+        copy = remote(src, dst.at[other], w_s.at[i], w_r.at[i], pair)
         copy.start()
         weights.append(copy)
 
@@ -306,11 +324,10 @@
 
     ld_c.wait()
     conv_back(x_v, act, w_c, mid)
-    normalize(mid, 0, attn)
+    normalize(mid, 0, ROWS // 128, attn)
 
     ld_k.wait()
     ld_v.wait()
-    ld_f.wait()
     for copy in weights[:3]:
         copy.wait()
 
@@ -321,7 +338,7 @@
         st_own[e] = s
 
     def keys(half, c, emit):
-        key_states(half, c, attn, wk_v, wv_v, fm_v, fmt, proj, val, kmapt, emit)
+        key_states(half, c, attn, wk_v, wv_v, fmt, val, kmapt, emit)
 
     def queries(half, c):
         intra(half, c, attn, wq_v, fm_v, proj, qmap, kmapt, val, num)
@@ -357,14 +374,14 @@
             chip_state = (st_own[e] + p_recv[e].astype(F32)).astype(BF16)
             a_send[c, i * per : (i + 1) * per] = chip_state.reshape(per, piece, HD)
 
-        @pl.loop(1, planes)
+        @pl.loop(1, planes, unroll=True)
         def _(k):
             a_copy(c, k).start()
 
         a_recv[c, plane] = a_send[c, plane]
 
     def y_start(c):
-        @pl.loop(1, planes)
+        @pl.loop(1, planes, unroll=True)
         def _(k):
             a_copy(c, k).wait()
 
@@ -396,14 +413,14 @@
             r_send[c, p] = run.astype(BF16)
             run = run + a_recv[c, p].astype(F32)
 
-        @pl.loop(1, planes)
+        @pl.loop(1, planes, unroll=True)
         def _(k):
             r_copy(c, k).start()
 
         r_recv[c, plane] = r_send[c, plane]
 
     def q_start(c):
-        @pl.loop(1, planes)
+        @pl.loop(1, planes, unroll=True)
         def _(k):
             r_copy(c, k).wait()
 
@@ -416,36 +433,39 @@
 
     keys(other, 0, emit_other)
     p_copy(0).start()
+    keys(own, 0, emit_own)
+    a_start(0)
     keys(other, 1, emit_other)
     p_copy(1).start()
-    keys(h, 0, emit_own)
-    a_start(0)
-    keys(h, 1, emit_own)
+    keys(own, 1, emit_own)
     a_start(1)
     ld_q.wait()
     ld_o.wait()
-    weights[3].wait()
-    weights[4].wait()
+    for copy in weights[3:]:
+        copy.wait()
     queries(other, 0)
     y_start(0)
     queries(other, 1)
     y_start(1)
     r_start(0)
-    queries(h, 0)
+    queries(own, 0)
     r_start(1)
-    queries(h, 1)
+    queries(own, 1)
     q_start(0)
-    inter(h, 0, qmap, pref, num, attended)
-    inter(h, 1, qmap, pref, num, attended)
+    inter(own, 0, qmap, pref, num, attended)
+    inter(own, 1, qmap, pref, num, attended)
+    q_copy(0).wait()
+    inter(other, 0, qmap, q_recv, num, attended)
+    inter(other, 1, qmap, q_recv, num, attended)
+    first_output(mid, attended, wo_v, acc)
     q_start(1)
-    inter(h, 2, qmap, pref, num, attended)
-    inter(h, 3, qmap, pref, num, attended)
-    first_output(h, mid, attended, wo_v, acc)
-    for c in range(2):
-        q_copy(c).wait()
-        for i in range(2):
-            inter(other, 2 * c + i, qmap, q_recv, num, attended)
-    last_output(other, acc, attended, wo_v, out)
+    inter(own, 2, qmap, pref, num, attended)
+    inter(own, 3, qmap, pref, num, attended)
+    own_output(own, attended, wo_v, acc)
+    q_copy(1).wait()
+    inter(other, 2, qmap, q_recv, num, attended)
+    inter(other, 3, qmap, q_recv, num, attended)
+    last_output(other, attended, wo_v, acc, out)
 
 
 def shards(sizes, *args):
@@ -477,7 +497,7 @@
         pltpu.VMEM((2, HEADS, ROWS, HD), F32),
         pltpu.VMEM((2, HEADS, ROWS, FEAT), BF16),
         pltpu.VMEM((ROWS, D), F32),
-        pltpu.VMEM((ROWS, HALF), BF16),
+        pltpu.VMEM((2, ROWS, HALF), BF16),
         pltpu.VMEM(state, F32),
         pltpu.VMEM(state, BF16),
         pltpu.VMEM(state, BF16),
@@ -490,11 +510,11 @@
         pltpu.VMEM(state, BF16),
         pltpu.VMEM(state, BF16),
         pltpu.VMEM(state, BF16),
-        dma((16,)),
+        dma((17,)),
         dma((2,)),
         dma((2,)),
-        dma((5,)),
-        dma((5,)),
+        dma((6,)),
+        dma((6,)),
         dma((2,)),
         dma((2,)),
         dma((2, planes)),

time: 41.3 us -> 39.9 us (0.966)
  Pallas kernels: 40.3 us -> 38.8 us
    pallas_call x1, Pallas kernels: 40.3 us -> 38.8 us  [shards(): pl.pallas_call(functools.partial(kernel, sizes), out_shape=pltpu.VMEM((RO...]
where the time goes in v3:
time: 39.9 us; the launch traced here: 39.8 us
  Pallas kernels  38.8 us (97%)
  local copies, waits for them, and re-layouts  0.97 us (2%)
    pallas_call x1, Pallas kernels, shards(): pl.pallas_call(functools.partial(kernel, sizes), out_shape=pltpu.VMEM((RO...  38.8 us
    unnamed x1, local copies, waits for them, and re-layouts  0.97 us

profile of v3, /device:TPU:25, one launch (start us, length us, event | category | flops | bytes accessed | tf_op | source)
XLA Modules:
  0.0 39.8 jit_solution(13517416811835584627)
XLA Ops:
  0.0 38.8 %block.1 = bf16[512,1024]{1,0:T(8,128)(2,1)S(1)} custom-call(bf16[512,1024]{1,0:T(8,128)(2,1)} %frames.1, bf16[1024,2048]{1,0:T(8,128)(2,1)} %conv_in.1, f32[31,1024]{1,0:T(8,128)} %taps.1, bf16[1024,1024]{1,0:T(8,128)(2,1)} %conv_out.1, bf16[1024,512]{1,0:T(8,128)(2,1)} %wq.1, bf16[1024,512]{1,0:T(8,128)(2,1)} %wk.1, bf16[1024,512]{1,0:T(8,128)(2,1)} %wv.1, ...), custom_call_target="tpu_custom_call" | custom-call | flops 10200000512 | bytes 13000000 | tf_op jit(solution)/shard_map/block/pallas_call | solution.py:529
  38.8 1.0 %copy.11 = bf16[512,1024]{1,0:T(8,128)(2,1)} copy(bf16[512,1024]{1,0:T(8,128)(2,1)S(1)} %block.1) | data formatting | bytes 2097152

commit v4 on v3

--- a/solution.py
+++ b/solution.py
@@ -209,9 +209,14 @@
     prev = device(lax.rem(lin + count - 1, count))
     following = device(lax.rem(lin + 1, count))
 
-    def plane_peer(k):
-        p = lax.rem(plane + k, planes)
-        return (y, lax.div(p, nz), lax.rem(p, nz), h)
+    def hops(offset):
+        return sum(min(d, n - d) for d, n in zip(offset, (nx, nz)))
+
+    offsets = [(i, j) for i in range(nx) for j in range(nz) if i or j]
+    offsets.sort(key=hops, reverse=True)
+
+    def plane_peer(offset):
+        return (y, lax.rem(x + offset[0], nx), lax.rem(z + offset[1], nz), h)
 
     loads = []
 
@@ -244,8 +249,7 @@
 
     greet(pair)
 
-    @pl.loop(1, planes)
-    def _(k):
+    for k in offsets:
         greet(plane_peer(k))
 
     for k in range(1, ny):
@@ -355,12 +359,14 @@
         return remote(q_send.at[at], q_recv.at[at], q_s.at[c], q_r.at[c], pair)
 
     def a_copy(c, k):
-        p = lax.rem(plane + k, planes)
-        return remote(a_send.at[c, p], a_recv.at[c, plane], a_s.at[c, k], a_r.at[c, k], plane_peer(k))
+        peer = plane_peer(k)
+        p = peer[1] * nz + peer[2]
+        return remote(a_send.at[c, p], a_recv.at[c, plane], a_s.at[c], a_r.at[c], peer)
 
     def r_copy(c, k):
-        p = lax.rem(plane + k, planes)
-        return remote(r_send.at[c, p], r_recv.at[c, plane], r_s.at[c, k], r_r.at[c, k], plane_peer(k))
+        peer = plane_peer(k)
+        p = peer[1] * nz + peer[2]
+        return remote(r_send.at[c, p], r_recv.at[c, plane], r_s.at[c], r_r.at[c], peer)
 
     def y_copy(c, k):
         return remote(
@@ -374,16 +380,17 @@
             chip_state = (st_own[e] + p_recv[e].astype(F32)).astype(BF16)
             a_send[c, i * per : (i + 1) * per] = chip_state.reshape(per, piece, HD)
 
-        @pl.loop(1, planes, unroll=True)
-        def _(k):
+        for k in offsets:
             a_copy(c, k).start()
 
         a_recv[c, plane] = a_send[c, plane]
 
     def y_start(c):
-        @pl.loop(1, planes, unroll=True)
-        def _(k):
-            a_copy(c, k).wait()
+        every = pl.ds(0, planes - 1)
+        pieces = remote(
+            a_send.at[c, every], a_recv.at[c, every], a_s.at[c], a_r.at[c], plane_peer(offsets[0])
+        )
+        pieces.wait()
 
         run = a_recv[c, 0].astype(F32)
         for p in range(1, planes):
@@ -413,16 +420,17 @@
             r_send[c, p] = run.astype(BF16)
             run = run + a_recv[c, p].astype(F32)
 
-        @pl.loop(1, planes, unroll=True)
-        def _(k):
+        for k in offsets:
             r_copy(c, k).start()
 
         r_recv[c, plane] = r_send[c, plane]
 
     def q_start(c):
-        @pl.loop(1, planes, unroll=True)
-        def _(k):
-            r_copy(c, k).wait()
+        every = pl.ds(0, planes - 1)
+        pieces = remote(
+            r_send.at[c, every], r_recv.at[c, every], r_s.at[c], r_r.at[c], plane_peer(offsets[0])
+        )
+        pieces.wait()
 
         for i in range(2):
             e = 2 * c + i
@@ -517,12 +525,12 @@
         dma((6,)),
         dma((2,)),
         dma((2,)),
-        dma((2, planes)),
-        dma((2, planes)),
+        dma((2,)),
+        dma((2,)),
         dma((2, ny)),
         dma((2, ny)),
-        dma((2, planes)),
-        dma((2, planes)),
+        dma((2,)),
+        dma((2,)),
         dma((2,)),
         dma((2,)),
     ]

time: 39.9 us -> 38 us (0.952)
  Pallas kernels: 38.8 us -> 36.9 us
    pallas_call x1, Pallas kernels: 38.8 us -> 36.9 us  [shards(): pl.pallas_call(functools.partial(kernel, sizes), out_shape=pltpu.VMEM((RO...]
where the time goes in v4:
time: 38 us; the launch traced here: 37.9 us
  Pallas kernels  36.9 us (97%)
  local copies, waits for them, and re-layouts  0.97 us (3%)
    pallas_call x1, Pallas kernels, shards(): pl.pallas_call(functools.partial(kernel, sizes), out_shape=pltpu.VMEM((RO...  36.9 us
    unnamed x1, local copies, waits for them, and re-layouts  0.97 us

profile of v4, /device:TPU:25, one launch (start us, length us, event | category | flops | bytes accessed | tf_op | source)
XLA Modules:
  0.0 37.9 jit_solution(3360417066871131514)
XLA Ops:
  0.0 36.9 %block.1 = bf16[512,1024]{1,0:T(8,128)(2,1)S(1)} custom-call(bf16[512,1024]{1,0:T(8,128)(2,1)} %frames.1, bf16[1024,2048]{1,0:T(8,128)(2,1)} %conv_in.1, f32[31,1024]{1,0:T(8,128)} %taps.1, bf16[1024,1024]{1,0:T(8,128)(2,1)} %conv_out.1, bf16[1024,512]{1,0:T(8,128)(2,1)} %wq.1, bf16[1024,512]{1,0:T(8,128)(2,1)} %wk.1, bf16[1024,512]{1,0:T(8,128)(2,1)} %wv.1, ...), custom_call_target="tpu_custom_call" | custom-call | flops 10200000512 | bytes 13000000 | tf_op jit(solution)/shard_map/block/pallas_call | solution.py:537
  36.9 1.0 %copy.11 = bf16[512,1024]{1,0:T(8,128)(2,1)} copy(bf16[512,1024]{1,0:T(8,128)(2,1)S(1)} %block.1) | data formatting | bytes 2097152

commit v5 on v4

--- a/solution.py
+++ b/solution.py
@@ -104,9 +104,9 @@
         convolve(pl.multiple_of(i * (ROWS - 64), 64), 64, glu, tap_v, dw)
 
 
-def activate(dw, act):
-    for i in range(ROWS // 128):
-        at = slice(i * 128, (i + 1) * 128)
+def activate(first, last, dw, act):
+    for i in range(first, last, 64):
+        at = slice(i, i + 64)
 
         def read(c):
             return dw[at, c * 128 : (c + 1) * 128]
@@ -304,6 +304,7 @@
 
     ld_tap.wait()
     convolve_inner(glu, tap_v, dw)
+    activate(64, ROWS - 64, dw, act)
 
     @pl.when(has_prev)
     def _():
@@ -324,7 +325,8 @@
         glu[pl.ds(HALO + ROWS, HALO), :] = jnp.zeros((HALO, D), F32)
 
     convolve_edges(glu, tap_v, dw)
-    activate(dw, act)
+    activate(0, 64, dw, act)
+    activate(ROWS - 64, ROWS, dw, act)
 
     ld_c.wait()
     conv_back(x_v, act, w_c, mid)

time: 38 us -> 37.7 us (level)
  no operation moved by 1% of the time
where the time goes in v5:
time: 37.7 us; the launch traced here: 37.6 us
  Pallas kernels  36.6 us (97%)
  local copies, waits for them, and re-layouts  0.97 us (3%)
    pallas_call x1, Pallas kernels, shards(): pl.pallas_call(functools.partial(kernel, sizes), out_shape=pltpu.VMEM((RO...  36.6 us
    unnamed x1, local copies, waits for them, and re-layouts  0.97 us

profile of v5, /device:TPU:25, one launch (start us, length us, event | category | flops | bytes accessed | tf_op | source)
XLA Modules:
  0.0 37.6 jit_solution(18093599667390844686)
XLA Ops:
  0.0 36.6 %block.1 = bf16[512,1024]{1,0:T(8,128)(2,1)S(1)} custom-call(bf16[512,1024]{1,0:T(8,128)(2,1)} %frames.1, bf16[1024,2048]{1,0:T(8,128)(2,1)} %conv_in.1, f32[31,1024]{1,0:T(8,128)} %taps.1, bf16[1024,1024]{1,0:T(8,128)(2,1)} %conv_out.1, bf16[1024,512]{1,0:T(8,128)(2,1)} %wq.1, bf16[1024,512]{1,0:T(8,128)(2,1)} %wk.1, bf16[1024,512]{1,0:T(8,128)(2,1)} %wv.1, ...), custom_call_target="tpu_custom_call" | custom-call | flops 10200000512 | bytes 13000000 | tf_op jit(solution)/shard_map/block/pallas_call | solution.py:539
  36.6 1.0 %copy.11 = bf16[512,1024]{1,0:T(8,128)(2,1)} copy(bf16[512,1024]{1,0:T(8,128)(2,1)S(1)} %block.1) | data formatting | bytes 2097152
